TPU v7x, 128 devices: a whole 4x4x4 slice. The times are simulated.
128 devices in a mesh: dp: 4 (over y_lo, core), fsdp: 32 (over x, z, y_hi).
Axes of the slice: x: 4, y: 4 (y_hi: 2, y_lo: 2; y = y_hi * 2 + y_lo), z: 4, core: 2. Of those that a mesh axis runs over, the one named last changes fastest.
Arguments:
- normed: bfloat16 [65536, 8192], P(('dp', 'fsdp')), may hold values from -24 to 24
- queries: bfloat16 [65536, 4096], P(('dp', 'fsdp')), may hold values from -96 to 96, as said below
- keys: bfloat16 [65536, 512], P(('dp', 'fsdp')), may hold values from -4.5 to 4.5
- value_weight: bfloat16 [8192, 512], P('fsdp'), may hold values from -0.0625 to 0.0625
- iterate: float32 [8192, 512], P('fsdp'), may hold values from -6 to 6
- residual: float32 [8192, 512], P('fsdp'), may hold values from -6 to 6
- direction: float32 [8192, 512], P('fsdp'), may hold values from -6 to 6
- damping: float32 [1], replicated, may hold values from 0.05 to 0.5
Outputs:
- new_iterate: float32 [8192, 512], P('fsdp')
- new_residual: float32 [8192, 512], P('fsdp')
- new_direction: float32 [8192, 512], P('fsdp')
Inputs may be any that keep to these rules, and one draw needn't show every extreme that they name: `queries`: queries are of order one except for a few rows, which may be large multiples of an earlier key of their key-value head.
All inputs are finite; a program needn't handle non-finite values.
Results may differ from a plain program's by a relative error of at most 0.0043.
Values may be sent and summed in bfloat16 or wider, within the bound.
No kernel may reach another device: no remote copies, remote signals or barrier semaphores. Data moves between devices by JAX's collectives and lax.ppermute only.
A program may use at most 192 MiB of HBM per device.

v0:
```python
import math
import jax
import jax.numpy as jnp
from jax import lax
from jax.sharding import PartitionSpec as P

HD = 128
EPSILON = 1e-05


def group_pull(query_rows, key_rows, value_rows, tangent_rows, head_size):
    seq_len = query_rows.shape[0]
    per_group = query_rows.shape[1] // head_size
    queries_split = query_rows.reshape(seq_len, per_group, head_size)
    scores = jnp.einsum(
        "tjd,sd->jts", queries_split, key_rows, preferred_element_type=jnp.float32
    ) / math.sqrt(head_size)
    positions = lax.iota(jnp.int32, seq_len)
    causal = positions[:, None] >= positions[None, :]
    scores = jnp.where(causal, scores, -jnp.inf)
    highest = jnp.max(scores, axis=-1, keepdims=True)
    exps = jnp.exp(scores - highest)
    weights_soft = (exps / jnp.sum(exps, axis=-1, keepdims=True)).astype(jnp.bfloat16)
    outputs = jnp.einsum(
        "jts,sd->tjd", weights_soft, value_rows, preferred_element_type=jnp.float32
    )
    tangents = jnp.einsum(
        "jts,sd->tjd", weights_soft, tangent_rows, preferred_element_type=jnp.float32
    )
    inverse = lax.rsqrt(jnp.mean(outputs * outputs, axis=-1, keepdims=True) + EPSILON)
    normal_out = outputs * inverse

    def jacobian(vector):
        return (
            vector - normal_out * jnp.mean(normal_out * vector, axis=-1, keepdims=True)
        ) * inverse

    wback = jacobian(jacobian(tangents)).astype(jnp.bfloat16)
    return jnp.einsum(
        "jts,tjd->sd", weights_soft, wback, preferred_element_type=jnp.float32
    ).astype(jnp.bfloat16)


def body(normed, queries, keys, value_weight, iterate, residual, direction, damping):
    seq_len = normed.shape[0]
    kv_width = keys.shape[1]
    kv_heads = kv_width // HD
    per_group = queries.shape[1] // kv_width
    dir_half = direction.astype(jnp.bfloat16)
    columns = normed
    projected = jnp.dot(
        columns,
        lax.all_gather(value_weight, "fsdp", axis=0, tiled=True),
        preferred_element_type=jnp.float32,
    )
    tangent = jnp.dot(
        columns,
        lax.all_gather(dir_half, "fsdp", axis=0, tiled=True),
        preferred_element_type=jnp.float32,
    )
    projected = projected.astype(jnp.bfloat16)
    tangent = tangent.astype(jnp.bfloat16)
    pulled_parts = []
    for group_index in range(kv_heads):
        query_cols = queries[:, group_index * per_group * HD : (group_index + 1) * per_group * HD]
        lower = group_index * HD
        pulled_parts.append(
            group_pull(
                query_cols,
                keys[:, lower : lower + HD],
                projected[:, lower : lower + HD],
                tangent[:, lower : lower + HD],
                HD,
            )
        )
    pulled = jnp.concatenate(pulled_parts, axis=1)
    tokens_all = lax.axis_size("dp") * lax.axis_size("fsdp") * seq_len
    columns = normed
    shard_sum = lax.psum_scatter(
        jnp.dot(columns.T, pulled, preferred_element_type=jnp.float32),
        "fsdp",
        scatter_dimension=0,
        tiled=True,
    )
    summed = lax.psum(shard_sum, "dp")
    hessian_dir = summed / tokens_all + damping[0] * direction
    old_sq = lax.psum(jnp.sum(residual * residual), "fsdp")
    curv_sum = lax.psum(jnp.sum(direction * hessian_dir), "fsdp")
    step_size = old_sq / curv_sum
    new_iterate = iterate + step_size * direction
    new_residual = residual - step_size * hessian_dir
    new_sq = lax.psum(jnp.sum(new_residual * new_residual), "fsdp")
    new_direction = new_residual + new_sq / old_sq * direction
    return (new_iterate, new_residual, new_direction)


def solution(mesh):
    return jax.shard_map(
        body,
        mesh=mesh,
        in_specs=(
            P(("dp", "fsdp"), None),
            P(("dp", "fsdp"), None),
            P(("dp", "fsdp"), None),
            P("fsdp", None),
            P("fsdp", None),
            P("fsdp", None),
            P("fsdp", None),
            P(),
        ),
        out_specs=(P("fsdp", None), P("fsdp", None), P("fsdp", None)),
        check_vma=False,
    )
```

profile of v0, /device:TPU:16, one launch (start us, length us, event | category | flops | bytes accessed | tf_op | source)
XLA Modules:
  0.0 863.5 jit_solution(4124391215796967002)
XLA Ops:
  7.9 1.8 convert_element_type.46
  9.8 3.9 fusion.124
  13.7 2.3 copy.97
  16.0 1.4 copy.99
  18.5 7.2 fusion.125
  25.7 7.2 fusion.135
  33.0 7.2 fusion.130
  40.2 7.1 fusion.140
  47.3 7.2 divide_convert_fusion
  54.5 3.5 divide_convert_fusion.2
  58.3 3.4 divide_convert_fusion.1
  61.7 0.9 slice-done.5
  62.6 3.3 divide_convert_fusion.3
  65.9 49.1 %all-gather.5.cloned.1.call-done = bf16[8192,512]{1,0:T(8,128)(2,1)} async-done(((bf16[256,512]{1,0:T(8,128)(2,1)}), bf16[8192,512]{1,0:T(8,128)(2,1)}) %all-gather.5.cloned.1.call-update) | async-done | bytes 8388624 | tf_op jit(solution)/shard_map/all_gather | solution.py:53
  115.0 10.4 %convolution_convert_fusion = bf16[512,512]{1,0:T(8,128)(2,1)S(1)} fusion(bf16[512,8192]{1,0:T(8,128)(2,1)} %param.8, bf16[8192,512]{1,0:T(8,128)(2,1)} %all-gather.5.cloned.1.call-done), kind=kOutput, calls=%fused_computation.69 | convolution fusion | flops 4295229440 | bytes 17301504 | tf_op jit(solution)/shard_map/dot_general | solution.py:51
  126.2 94.4 %all-gather.3.cloned.1.call-done = bf16[8192,512]{1,0:T(8,128)(2,1)} async-done(((bf16[256,512]{1,0:T(8,128)(2,1)}), bf16[8192,512]{1,0:T(8,128)(2,1)}) %all-gather.3.cloned.1.call-update) | async-done | bytes 8388624 | tf_op jit(solution)/shard_map/all_gather | solution.py:58
  220.6 10.4 %convolution_convert_fusion.1 = bf16[512,512]{1,0:T(8,128)(2,1)S(1)} fusion(bf16[512,8192]{1,0:T(8,128)(2,1)} %param.8, bf16[8192,512]{1,0:T(8,128)(2,1)} %all-gather.3.cloned.1.call-done), kind=kOutput, calls=%fused_computation.70 | convolution fusion | flops 4295229440 | bytes 17301504 | tf_op jit(solution)/shard_map/dot_general | solution.py:56
  232.4 1.5 fusion.35
  236.8 1.3 fusion.33
  238.1 0.9 copy-done.1
  241.1 1.3 fusion.34
  245.5 1.3 fusion.32
  246.9 0.9 slice-done.1
  247.8 8.2 convolution_bitcast_fusion
  256.0 360.2 %reduce-scatter.2.cloned.1.call-done = f32[256,512]{0,1:T(8,128)} async-done(((f32[8192,512]{0,1:T(8,128)}), f32[256,512]{0,1:T(8,128)}) %reduce-scatter.2.cloned.1.call-update) | async-done | bytes 524304 | tf_op jit(solution)/shard_map/reduce_scatter | solution.py:79
  618.1 43.0 %all-reduce.3.cloned.1.call-done = f32[256,512]{0,1:T(8,128)} async-done(((f32[256,512]{0,1:T(8,128)}), f32[256,512]{0,1:T(8,128)}) %all-reduce.3.cloned.1.call-update) | async-done | bytes 524304 | tf_op jit(solution)/shard_map/psum | solution.py:85
  661.0 1.9 multiply_reduce_fusion.5
  663.1 90.6 %all-reduce = (f32[]{:T(128)}, f32[]{:T(128)}) all-reduce(f32[]{:T(128)} %multiply_reduce_fusion.6, f32[]{:T(128)} %multiply_reduce_fusion.5), channel_id=1, replica_groups=mesh['dp'=4,'fsdp'=32] {'fsdp'}, use_global_device_ids=true, to_apply=%region_1.2 | all-reduce | flops 2 | bytes 16 | tf_op jit(solution)/shard_map/psum | solution.py:87
  755.8 96.4 %psum.31 = f32[]{:T(128)} all-reduce(f32[]{:T(128)} %get-tuple-element.11), channel_id=1, replica_groups=mesh['dp'=4,'fsdp'=32] {'fsdp'}, use_global_device_ids=true, to_apply=%region_27.28 | all-reduce | flops 1 | bytes 8 | tf_op jit(solution)/shard_map/psum | solution.py:92
  853.5 1.0 copy.67
  854.6 1.0 copy.68
  855.6 1.0 copy.66
  (77 shorter events, 14.6 us)
Async XLA Ops:
  7.2 107.8 %all-gather.5.cloned.1.call-start = ((), (), s32[]{:S(2)}) async-start(), calls=%async_computation.2 | async-start | bytes 8650752 | tf_op jit(solution)/shard_map/all_gather | solution.py:53
  7.9 212.7 %all-gather.3.cloned.1.call-start = ((), (), s32[]{:S(2)}) async-start(), calls=%async_computation.1 | async-start | bytes 8650752 | tf_op jit(solution)/shard_map/all_gather | solution.py:58
  9.7 606.5 %reduce-scatter.2.cloned.1.call-start = ((), (), s32[]{:S(2)}) async-start(), calls=%async_computation.3 | async-start | bytes 17301504 | tf_op jit(solution)/shard_map/reduce_scatter | solution.py:79
  25.7 7.2 copy-start.10
  32.9 7.2 copy-start.9
  47.3 7.2 copy-start.5
  47.3 10.6 %slice-start.2 = ((s8[8388608]{0:T(1024)(128)(4,1)}), s8[4194304]{0:T(1024)(128)(4,1)S(1)}, s32[]{:S(2)}) async-start(s8[8388608]{0:T(1024)(128)(4,1)} %bitcast.284), calls=%async_computation.7 | async-start | bytes 8388608
  54.5 3.8 slice-start.3
  54.5 7.2 slice-start.4
  58.3 4.3 slice-start.5
  115.0 10.4 %copy-start.3 = (bf16[8,512,512]{1,2,0:T(8,128)(2,1)S(1)}, bf16[8,512,512]{1,2,0:T(8,128)(2,1)}, u32[]{:S(2)}) copy-start(bf16[8,512,512]{1,2,0:T(8,128)(2,1)} %divide_convert_fusion) | copy-start | bytes 12582916
  220.6 10.4 %copy-start.4 = (bf16[8,512,512]{1,2,0:T(8,128)(2,1)S(1)}, bf16[8,512,512]{1,2,0:T(8,128)(2,1)}, u32[]{:S(2)}) copy-start(bf16[8,512,512]{1,2,0:T(8,128)(2,1)} %divide_convert_fusion) | copy-start | bytes 12582916
  232.4 2.2 copy-start.2
  236.8 2.2 copy-start.1
  241.1 2.2 copy-start
  244.1 2.8 slice-start
  244.9 2.9 slice-start.1
  255.9 360.3 %copy-start.6 = (f32[256,512]{1,0:T(8,128)S(1)}, f32[256,512]{1,0:T(8,128)}, u32[]{:S(2)}) copy-start(f32[256,512]{1,0:T(8,128)} %param.14) | copy-start | bytes 1572868
  255.9 361.2 %copy-start.7 = (f32[256,512]{1,0:T(8,128)S(1)}, f32[256,512]{1,0:T(8,128)}, u32[]{:S(2)}) copy-start(f32[256,512]{1,0:T(8,128)} %param.13) | copy-start | bytes 1572868
  256.0 405.1 %all-reduce.3.cloned.1.call-start = ((), (), s32[]{:S(2)}) async-start(), calls=%async_computation.4 | async-start | bytes 1048576 | tf_op jit(solution)/shard_map/psum | solution.py:85
  616.2 46.7 %copy-start.11 = (f32[256,512]{1,0:T(8,128)S(1)}, f32[256,512]{1,0:T(8,128)}, u32[]{:S(2)}) copy-start(f32[256,512]{1,0:T(8,128)} %param.12) | copy-start | bytes 1572868
  661.0 94.0 %copy-start.8 = (f32[256,512]{0,1:T(8,128)S(1)}, f32[256,512]{0,1:T(8,128)}, u32[]{:S(2)}) copy-start(f32[256,512]{0,1:T(8,128)} %all-reduce.3.cloned.1.call-done) | copy-start | bytes 1572868
Sparse Core Ops, SparseCore 0:
  11.0 103.9 all-gather.4
  118.6 101.9 all-gather.2
  256.1 360.0 reduce-scatter.1
  618.6 42.4 all-reduce.2
where the time goes:
time: 874 us; the launch traced here: 864 us
  waiting for transfers between devices  547 us (63%)
  blocking collectives  187 us (21%)
  matrix products  69.3 us (8%)
  other arithmetic  25 us (3%)
  between operations  17.9 us (2%)
  local copies, waits for them, and re-layouts  16.8 us (2%)
    reduce_scatter x1, waiting for transfers between devices, body(): lax.psum_scatter(jnp.dot(columns.T, pulled, preferred_element_type=jnp.fl...  360 us
    psum x1, blocking collectives, body(): new_sq = lax.psum(jnp.sum(new_residual * new_residual), 'fsdp')  96.4 us
    all_gather x1, waiting for transfers between devices, body(): lax.all_gather(dir_half, 'fsdp', axis=0, tiled=True)  94.4 us
    psum x1, blocking collectives, body(): old_sq = lax.psum(jnp.sum(residual * residual), 'fsdp')  90.6 us
    all_gather x1, waiting for transfers between devices, body(): lax.all_gather(value_weight, 'fsdp', axis=0, tiled=True)  49.1 us
    psum x1, waiting for transfers between devices, body(): summed = lax.psum(shard_sum, 'dp')  43 us
    sub x4, matrix products, group_pull(): exps = jnp.exp(scores - highest)  28.8 us
  transfers between devices with their start and end apart: 4, of which 4 were waited for; matrix products, arithmetic and copies ran while one was open for 8% of the time, Pallas kernels for 0%

commit v1 on v0

--- a/solution.py
+++ b/solution.py
@@ -55,7 +55,9 @@
     )
     tangent = jnp.dot(
         columns,
-        lax.all_gather(dir_half, "fsdp", axis=0, tiled=True),
+        jnp.concatenate(
+            lax.all_to_all(jnp.stack([dir_half] * lax.axis_size("fsdp")), "fsdp", 0, 0), axis=0
+        ),
         preferred_element_type=jnp.float32,
     )
     projected = projected.astype(jnp.bfloat16)

time: 874 us -> 863 us (0.987)
  waiting for transfers between devices: 547 us -> 529 us
  starting transfers between devices: 0.16 us -> 11.1 us
    all_gather x1 -> x0, waiting for transfers between devices: 94.4 us -> none  [body(): lax.all_gather(dir_half, 'fsdp', axis=0, tiled=True)]
    all_to_all x0 -> x1, waiting for transfers between devices: none -> 77.2 us  [body(): lax.all_to_all(jnp.stack([dir_half] * lax.axis_size('fsdp')), 'fsdp', 0, 0)]
    all_to_all x0 -> x1, starting transfers between devices: none -> 10.9 us  [body(): lax.all_to_all(jnp.stack([dir_half] * lax.axis_size('fsdp')), 'fsdp', 0, 0)]
where the time goes in v1:
time: 863 us; the launch traced here: 859 us
  waiting for transfers between devices  529 us (61%)
  blocking collectives  187 us (22%)
  matrix products  69.4 us (8%)
  other arithmetic  24.3 us (3%)
  local copies, waits for them, and re-layouts  21.3 us (2%)
  between operations  17.7 us (2%)
  starting transfers between devices  11.1 us (1%)
    reduce_scatter x1, waiting for transfers between devices, body(): lax.psum_scatter(jnp.dot(columns.T, pulled, preferred_element_type=jnp.fl...  360 us
    psum x1, blocking collectives, body(): new_sq = lax.psum(jnp.sum(new_residual * new_residual), 'fsdp')  96.4 us
    psum x1, blocking collectives, body(): old_sq = lax.psum(jnp.sum(residual * residual), 'fsdp')  90.6 us
    all_to_all x1, waiting for transfers between devices, body(): lax.all_to_all(jnp.stack([dir_half] * lax.axis_size('fsdp')), 'fsdp', 0, 0)  77.2 us
    all_gather x1, waiting for transfers between devices, body(): lax.all_gather(value_weight, 'fsdp', axis=0, tiled=True)  47.3 us
    psum x1, waiting for transfers between devices, body(): summed = lax.psum(shard_sum, 'dp')  43.2 us
    sub x4, matrix products, group_pull(): exps = jnp.exp(scores - highest)  29.1 us
    convert_element_type x4, other arithmetic, group_pull(): (exps / jnp.sum(exps, axis=-1, keepdims=True)).astype(jnp.bfloat16)  17.3 us
  transfers between devices with their start and end apart: 4, of which 4 were waited for; matrix products, arithmetic and copies ran while one was open for 8% of the time, Pallas kernels for 0%

profile of v1, /device:TPU:16, one launch (start us, length us, event | category | flops | bytes accessed | tf_op | source)
XLA Modules:
  0.0 859.4 jit_solution(11687842627330032611)
XLA Ops:
  7.9 1.1 convert_element_type.46
  9.0 4.2 stack.2
  13.1 10.9 %all-to-all-start = ((bf16[32,256,512]{2,1,0:T(8,128)(2,1)}), bf16[32,256,512]{2,1,0:T(8,128)(2,1)}, u32[]{:S(2)}, u32[]{:S(2)}) async-start(bf16[32,256,512]{2,1,0:T(8,128)(2,1)} %stack.2), calls=%async_computation | async-start | bytes 16777216 | tf_op jit(solution)/shard_map/all_to_all | solution.py:59
  24.2 3.9 fusion.124
  28.1 2.3 copy.97
  30.4 1.3 copy.98
  32.3 1.0 copy.100
  33.4 7.6 fusion.140
  41.0 7.1 fusion.135
  48.2 7.1 fusion.130
  55.3 7.2 fusion.125
  62.5 7.1 divide_convert_fusion.3
  69.6 3.5 divide_convert_fusion.2
  73.1 3.5 divide_convert_fusion.1
  76.5 1.1 slice-done.5
  77.6 3.3 divide_convert_fusion
  80.9 77.2 %all-to-all-done = bf16[32,256,512]{2,1,0:T(8,128)(2,1)} async-done(((bf16[32,256,512]{2,1,0:T(8,128)(2,1)}), bf16[32,256,512]{2,1,0:T(8,128)(2,1)}, u32[]{:S(2)}, u32[]{:S(2)}) %all-to-all-start) | async-done | bytes 8388640 | tf_op jit(solution)/shard_map/all_to_all | solution.py:59
  158.1 10.2 %convolution_convert_fusion.1 = bf16[512,512]{1,0:T(8,128)(2,1)S(1)} fusion(bf16[512,8192]{1,0:T(8,128)(2,1)} %param.8, bf16[8192,512]{1,0:T(8,128)(2,1)} %bitcast.3), kind=kOutput, calls=%fused_computation.70 | convolution fusion | flops 4295229440 | bytes 17301504 | tf_op jit(solution)/shard_map/dot_general | solution.py:56
  168.3 47.3 %all-gather.2.cloned.1.call-done = bf16[8192,512]{1,0:T(8,128)(2,1)} async-done(((bf16[256,512]{1,0:T(8,128)(2,1)}), bf16[8192,512]{1,0:T(8,128)(2,1)}) %all-gather.2.cloned.1.call-update) | async-done | bytes 8388624 | tf_op jit(solution)/shard_map/all_gather | solution.py:53
  215.6 10.4 %convolution_convert_fusion = bf16[512,512]{1,0:T(8,128)(2,1)S(1)} fusion(bf16[512,8192]{1,0:T(8,128)(2,1)} %param.8, bf16[8192,512]{1,0:T(8,128)(2,1)} %all-gather.2.cloned.1.call-done), kind=kOutput, calls=%fused_computation.69 | convolution fusion | flops 4295229440 | bytes 17301504 | tf_op jit(solution)/shard_map/dot_general | solution.py:51
  228.2 1.5 fusion.32
  232.6 1.3 fusion.33
  237.0 1.3 fusion.34
  241.4 1.3 fusion.35
  243.6 8.2 convolution_bitcast_fusion
  251.9 360.2 %reduce-scatter.2.cloned.1.call-done = f32[256,512]{0,1:T(8,128)} async-done(((f32[8192,512]{0,1:T(8,128)}), f32[256,512]{0,1:T(8,128)}) %reduce-scatter.2.cloned.1.call-update) | async-done | bytes 524304 | tf_op jit(solution)/shard_map/reduce_scatter | solution.py:81
  613.9 43.2 %all-reduce.3.cloned.1.call-done = f32[256,512]{0,1:T(8,128)} async-done(((f32[256,512]{0,1:T(8,128)}), f32[256,512]{0,1:T(8,128)}) %all-reduce.3.cloned.1.call-update) | async-done | bytes 524304 | tf_op jit(solution)/shard_map/psum | solution.py:87
  657.1 1.9 multiply_reduce_fusion.5
  659.2 90.6 %all-reduce = (f32[]{:T(128)}, f32[]{:T(128)}) all-reduce(f32[]{:T(128)} %multiply_reduce_fusion.6, f32[]{:T(128)} %multiply_reduce_fusion.5), channel_id=1, replica_groups=mesh['dp'=4,'fsdp'=32] {'fsdp'}, use_global_device_ids=true, to_apply=%region_1.2 | all-reduce | flops 2 | bytes 16 | tf_op jit(solution)/shard_map/psum | solution.py:89
  751.8 96.4 %psum.31 = f32[]{:T(128)} all-reduce(f32[]{:T(128)} %get-tuple-element.11), channel_id=1, replica_groups=mesh['dp'=4,'fsdp'=32] {'fsdp'}, use_global_device_ids=true, to_apply=%region_27.28 | all-reduce | flops 1 | bytes 8 | tf_op jit(solution)/shard_map/psum | solution.py:94
  849.6 1.0 copy.67
  850.7 1.0 copy.66
  (73 shorter events, 16.5 us)
Async XLA Ops:
  7.2 208.5 %all-gather.2.cloned.1.call-start = ((), (), s32[]{:S(2)}) async-start(), calls=%async_computation.2 | async-start | bytes 8650752 | tf_op jit(solution)/shard_map/all_gather | solution.py:53
  13.1 145.0 %all-to-all-start = ((bf16[32,256,512]{2,1,0:T(8,128)(2,1)}), bf16[32,256,512]{2,1,0:T(8,128)(2,1)}, u32[]{:S(2)}, u32[]{:S(2)}) async-start(bf16[32,256,512]{2,1,0:T(8,128)(2,1)} %stack.2), calls=%async_computation | async-start | bytes 16777216 | tf_op jit(solution)/shard_map/all_to_all | solution.py:59
  24.1 588.0 %reduce-scatter.2.cloned.1.call-start = ((), (), s32[]{:S(2)}) async-start(), calls=%async_computation.3 | async-start | bytes 17301504 | tf_op jit(solution)/shard_map/reduce_scatter | solution.py:81
  33.4 7.6 copy-start.8
  62.5 7.1 copy-start.4
  62.5 10.6 %slice-start.2 = ((s8[8388608]{0:T(1024)(128)(4,1)}), s8[4194304]{0:T(1024)(128)(4,1)S(1)}, s32[]{:S(2)}) async-start(s8[8388608]{0:T(1024)(128)(4,1)} %bitcast.285), calls=%async_computation.7 | async-start | bytes 8388608
  69.6 3.5 slice-start.3
  69.6 6.9 slice-start.4
  73.1 4.5 slice-start.5
  215.6 10.4 %copy-start.3 = (bf16[8,512,512]{1,2,0:T(8,128)(2,1)S(1)}, bf16[8,512,512]{1,2,0:T(8,128)(2,1)}, u32[]{:S(2)}) copy-start(bf16[8,512,512]{1,2,0:T(8,128)(2,1)} %divide_convert_fusion.3) | copy-start | bytes 12582916
  228.2 2.2 copy-start.2
  232.6 2.2 copy-start.1
  237.0 2.2 copy-start
  239.9 2.8 slice-start
  240.8 2.9 slice-start.1
  251.8 360.3 %copy-start.5 = (f32[256,512]{1,0:T(8,128)S(1)}, f32[256,512]{1,0:T(8,128)}, u32[]{:S(2)}) copy-start(f32[256,512]{1,0:T(8,128)} %param.14) | copy-start | bytes 1572868
  251.8 361.2 %copy-start.6 = (f32[256,512]{1,0:T(8,128)S(1)}, f32[256,512]{1,0:T(8,128)}, u32[]{:S(2)}) copy-start(f32[256,512]{1,0:T(8,128)} %param.13) | copy-start | bytes 1572868
  251.8 405.3 %all-reduce.3.cloned.1.call-start = ((), (), s32[]{:S(2)}) async-start(), calls=%async_computation.4 | async-start | bytes 1048576 | tf_op jit(solution)/shard_map/psum | solution.py:87
  612.1 46.9 %copy-start.9 = (f32[256,512]{1,0:T(8,128)S(1)}, f32[256,512]{1,0:T(8,128)}, u32[]{:S(2)}) copy-start(f32[256,512]{1,0:T(8,128)} %param.12) | copy-start | bytes 1572868
  657.1 94.0 %copy-start.7 = (f32[256,512]{0,1:T(8,128)S(1)}, f32[256,512]{0,1:T(8,128)}, u32[]{:S(2)}) copy-start(f32[256,512]{0,1:T(8,128)} %all-reduce.3.cloned.1.call-done) | copy-start | bytes 1572868
Sparse Core Ops, SparseCore 0:
  11.0 204.5 all-gather.1
  251.9 360.0 reduce-scatter.1
  614.6 42.4 all-reduce.2
